TPU v7x, 32 devices: a whole 2x2x4 slice. The times are simulated.
32 devices in a mesh: region: 8 (over y, x, core), row: 4 (over z).
Axes of the slice: x: 2, y: 2, z: 4, core: 2. Of those that a mesh axis runs over, the one named last changes fastest.
Arguments:
- inputs: bfloat16 [12, 16384, 227], P('row', 'region'), may hold values from -6 to 6
- targets: bfloat16 [12, 16384, 227], P('row', 'region'), may hold values from -6 to 6
- valid_steps: int32 [12, 16384], P('row', 'region'), may hold values from 0 to 1, as said below
- var_weights: float32 [227], replicated, may hold values from 0.3 to 3
- grid_to_mesh: int32 [4096, 4], P('region'), may hold values from 0 to 2047
- mesh_edges: int32 [4096, 8], P('region'), may hold values from 0 to 639
- send_rows: int32 [1024], P('region'), may hold values from 0 to 511
- mesh_to_grid: int32 [16384, 3], P('region'), may hold values from 0 to 511
- date_index: int32 [12], P('row'), may hold values from 0 to 7
- matrices: float32 [7, 512, 512], P(None, 'row'), may hold values from -0.25 to 0.25
- matrices_momentum: float32 [7, 512, 512], P(None, 'row'), may hold values from -0.125 to 0.125
- in_proj: float32 [227, 512], P(None, 'row'), may hold values from -0.375 to 0.375
- in_first: float32 [227, 512], P(None, 'row'), may hold values from -0.015625 to 0.015625
- in_second: float32 [227, 512], P(None, 'row'), may hold values from 2.1362305e-06 to 3.4077962e-05
- out_proj: float32 [512, 227], P('row'), may hold values from -0.25 to 0.25
- out_first: float32 [512, 227], P('row'), may hold values from -0.015625 to 0.015625
- out_second: float32 [512, 227], P('row'), may hold values from 2.1362305e-06 to 3.4077962e-05
- norm_gains: float32 [3, 512], P(None, 'row'), may hold values from 0.5 to 1.5
- gains_first: float32 [3, 512], P(None, 'row'), may hold values from -0.046875 to 0.046875
- gains_second: float32 [3, 512], P(None, 'row'), may hold values from 1.93278e-05 to 0.00030517578
- date_table: float32 [8, 512], P(None, 'row'), may hold values from -3 to 3
- date_first: float32 [8, 512], P(None, 'row'), may hold values from -0.046875 to 0.046875
- date_second: float32 [8, 512], P(None, 'row'), may hold values from 1.93278e-05 to 0.00030517578
Outputs:
- new_matrices: float32 [7, 512, 512], P(None, 'row')
- new_momentum: float32 [7, 512, 512], P(None, 'row')
- new_in_proj: float32 [227, 512], P(None, 'row')
- new_in_first: float32 [227, 512], P(None, 'row')
- new_in_second: float32 [227, 512], P(None, 'row')
- new_out_proj: float32 [512, 227], P('row')
- new_out_first: float32 [512, 227], P('row')
- new_out_second: float32 [512, 227], P('row')
- new_gains: float32 [3, 512], P(None, 'row')
- new_gains_first: float32 [3, 512], P(None, 'row')
- new_gains_second: float32 [3, 512], P(None, 'row')
- new_dates: float32 [8, 512], P(None, 'row')
- new_date_first: float32 [8, 512], P(None, 'row')
- new_date_second: float32 [8, 512], P(None, 'row')
- loss_sum: float32 [], replicated
- valid_count: float32 [], replicated
Inputs may be any that keep to these rules, and one draw needn't show every extreme that they name: `valid_steps`: each value is 0 or 1; the share of ones varies over members and grid points. `grid_to_mesh`: indices of grid points within the mesh node's own region. `mesh_edges`: rows below 512 are the region's own mesh nodes; the next 64 rows come from the previous region, the last 64 from the next one, cyclically. `send_rows`: within a region's 2 * 64 slots, the first 64 go to the previous region and the last 64 to the next one; a row may be sent several times. `mesh_to_grid`: indices of mesh nodes within the grid point's own region.
All inputs are finite; a program needn't handle non-finite values.
Results may differ from a plain program's by a relative error of at most 0.0011.
The roundings to bfloat16 on the way count: a program that leaves them out, or rounds other values in their place, can miss the bound.
Values may be sent and summed in bfloat16 or wider, within the bound.
A program may use at most 320 MiB of HBM per device.

v0:
```python
from functools import partial

import jax
import jax.numpy as jnp
from jax import lax
from jax.experimental import pallas as pl
from jax.experimental.pallas import tpu as pltpu
from jax.sharding import PartitionSpec as P

NS_ITERS = 2
STEP = 10
NS_COEFFS = (3.4445, -4.775, 2.0315)
MUON_RATE = 0.8
MUON_MOMENTUM = 0.95
MATRIX_RATE = 0.05
VECTOR_RATE = 0.2
BETA_ONE = 0.9
BETA_TWO = 0.95
WEIGHT_DECAY = 0.01

F32 = jnp.float32
BF16 = jnp.bfloat16
LATENT = 512
BLOCK = 1024
PARTS = 1
T_TYPE = BF16
VMEM_BYTES = 60 * 1024 * 1024
MESH = pl.DeviceIdType.MESH
SLOTS = 8
SMALL = 6
IN_ROW, OUT_ROW, GAIN_ROW, DATE_ROW, LOSS_ROW = 0, 240, 480, 496, 504


def dot(left, right):
    return jnp.dot(left, right, preferred_element_type=F32)


def dot_nt(left, right):
    return lax.dot_general(left, right, (((1,), (1,)), ((), ())), preferred_element_type=F32)


def dot_tn(left, right):
    return lax.dot_general(left, right, (((0,), (0,)), ((), ())), preferred_element_type=F32)


def split_two(values):
    high = values.astype(BF16)
    return high, (values - high.astype(F32)).astype(BF16)


def silu_parts(half):
    bend = jnp.tanh(half)
    gate = 0.5 * bend + 0.5
    hid = half * bend + half
    return hid, gate + hid * (1.0 - gate)


def normalise(values):
    centred = values - jnp.mean(values, axis=-1, keepdims=True)
    spread = jnp.mean(centred * centred, axis=-1, keepdims=True)
    scale = lax.rsqrt(spread + 1e-05)
    return centred * scale, scale


def norm_back(grad, gain, unit, scale):
    scaled = gain * grad
    mean_one = jnp.mean(scaled, axis=-1, keepdims=True)
    mean_two = jnp.mean(scaled * unit, axis=-1, keepdims=True)
    return scale * (scaled - mean_one - unit * mean_two)


def in_turn(parts):
    parts = list(parts)
    while parts:
        parts = [part for part in parts if next(part, None) is not None]


def count_columns(index, width, count):
    lanes = lax.broadcasted_iota(jnp.int32, (index.shape[0], width), 1)
    total = None
    for k in range(count):
        one = jnp.where(lanes == index[:, k : k + 1], 1.0, 0.0)
        total = one if total is None else total + one
    return total.astype(BF16)


def gain_row(small_ref, k):
    return small_ref[GAIN_ROW : GAIN_ROW + 16, :].astype(F32)[k : k + 1, :]


def date_row(small_ref, day):
    table = small_ref[DATE_ROW : DATE_ROW + 16, :].astype(F32)
    lines = lax.broadcasted_iota(jnp.int32, table.shape, 0)
    return jnp.sum(jnp.where(lines == day, table, 0.0), axis=0, keepdims=True)


def columns_of(index):
    short = 8 - index.shape[0]
    if short > 0:
        index = jnp.concatenate([index, jnp.zeros((short, index.shape[1]), index.dtype)], axis=0)
    return jnp.transpose(index)


def count_rows(index, height):
    lines = lax.broadcasted_iota(jnp.int32, (height, index.shape[1]), 0)
    total = None
    for k in range(index.shape[0]):
        one = jnp.where(lines == index[k : k + 1, :], 1.0, 0.0)
        total = one if total is None else total + one
    return total.astype(BF16)


def main_kernel(
    k_pick, day_ref, mesh_ref, sent_ref, left_ref, right_ref, x_ref, y_ref, valid_ref, varw_ref,
    eh_in, eht_in, d_in, dt_in, small_ref, m2_ref, m3_ref, m4_ref, m5_ref, m6_ref,
    slots_ref, gout_ref, gxd_ref, dsum_ref, ggain_ref, loss_ref, dmesh_ref, dhalo_ref,
    gm_ref, out_sem, in_sem, eh_ref, eht_ref, d_ref, dt_ref, ext_ref, t_ref, mm_ref, acc_ref, sender_ref,
):
    nodes = mesh_ref.shape[1]
    table = ext_ref.shape[0]
    variables, points = x_ref.shape[1:]
    k_edge = eh_ref.shape[0] // nodes
    counts = [
        pltpu.make_async_copy(source, target, in_sem.at[k])
        for k, (source, target) in enumerate(
            ((eh_in, eh_ref), (d_in, d_ref), (dt_in, dt_ref), (eht_in, eht_ref))
        )
    ]

    def counts_ready(*which):
        @pl.when(pl.program_id(0) == 0)
        def _():
            for k in which:
                counts[k].wait()

    halo = left_ref.shape[1]

    @pl.when(pl.program_id(0) == 0)
    def _():
        for copy in counts:
            copy.start()
        gm_ref[...] = jnp.zeros_like(gm_ref)
        gout_ref[...] = jnp.zeros_like(gout_ref)
        gxd_ref[...] = jnp.zeros_like(gxd_ref)
        ggain_ref[...] = jnp.zeros_like(ggain_ref)
        loss_ref[...] = jnp.zeros_like(loss_ref)

    sent = sent_ref[0]
    ext_ref[:nodes, :] = sent
    ext_ref[nodes : nodes + halo, :] = left_ref[0]
    ext_ref[nodes + halo :, :] = right_ref[0]
    receivers = 0.5 * dot(sent, m3_ref[0])
    sender_ref[...] = (0.5 * dot(ext_ref[...], m2_ref[0])).astype(BF16)

    counts_ready(0)

    def edge(k, carry):
        hid_sum, t_sum = carry
        rows = pl.ds(pl.multiple_of(k * nodes, nodes), nodes)
        hid, t = silu_parts(1.0 * dot(eh_ref[rows, :], sender_ref[...]) + receivers)
        t_ref[rows, :] = t.astype(t_ref.dtype)
        return hid_sum + hid.astype(BF16).astype(F32), t_sum + t

    zero = jnp.zeros((nodes, LATENT), F32)
    hid_sum, t_sum = lax.fori_loop(0, k_edge, edge, (zero, zero), unroll=k_edge)
    h_high = (hid_sum * (1.0 / k_edge)).astype(BF16)
    gain2 = gain_row(small_ref, 1)
    unit2, scale2 = normalise(dot(h_high, m4_ref[0]))
    mesh2 = mesh_ref[0] + unit2 * gain2
    mm_ref[...] = mesh2.astype(BF16)

    counts_ready(1, 2)
    acc_ref[...] = jnp.zeros_like(acc_ref)
    dsum_ref[...] = jnp.zeros_like(dsum_ref)
    member = pl.program_id(0)
    date = date_row(small_ref, day_ref[member])
    gain3 = gain_row(small_ref, 2)
    wout = small_ref[OUT_ROW : OUT_ROW + variables, :]
    square = (variables, variables)
    same = lax.broadcasted_iota(jnp.int32, square, 0) == lax.broadcasted_iota(jnp.int32, square, 1)
    varw = jnp.sum(jnp.where(same, varw_ref[...], 0.0), axis=1, keepdims=True)

    def decode_part(rows):
        dec = dot(d_ref[rows, :], mm_ref[...])
        a2 = (dec * (1.0 / k_pick)).astype(BF16)
        yield True
        hid, t = silu_parts(0.5 * dot(a2, m5_ref[0]))
        h2 = hid.astype(BF16)
        yield True
        unit, scale = normalise(dot(h2, m6_ref[0]))
        yield True
        x = x_ref[0, :, rows]
        grid = dot_tn(x, small_ref[IN_ROW : IN_ROW + variables, :]) + date + unit * gain3
        grid = grid.astype(BF16)
        yield True
        misfit = x.astype(F32) + dot_nt(wout, grid) - y_ref[0, :, rows].astype(F32)
        valid = valid_ref[pl.ds(member, 1), rows].astype(F32)
        weighted = valid * varw * misfit
        loss_ref[...] += jnp.sum(weighted * misfit, axis=1, keepdims=True)
        dsum_ref[0] += jnp.sum(weighted, axis=1, keepdims=True)
        dp = weighted.astype(BF16)
        gout_ref[...] += dot(dp, grid)
        gxd_ref[...] += dot_nt(x, dp)
        yield True
        dgrid = dot_tn(dp, wout)
        ggain_ref[1:2, :] += jnp.sum(dgrid * unit, axis=0, keepdims=True)
        dc = norm_back(dgrid, gain3, unit, scale).astype(BF16)
        gm_ref[4] += dot_tn(h2, dc)
        yield True
        du = (dot_nt(dc, m6_ref[0]) * t).astype(BF16)
        gm_ref[3] += dot_tn(a2, du)
        yield True
        ddec = dot_nt(du, m5_ref[0]).astype(BF16)
        acc_ref[...] += dot(dt_ref[:, rows], ddec)
        yield True

    def grid_block(i, carry):
        part = BLOCK // PARTS
        in_turn(
            decode_part(pl.ds(pl.multiple_of(i * BLOCK + k * part, part), part)) for k in range(PARTS)
        )
        return carry

    lax.fori_loop(0, points // BLOCK, grid_block, 0)

    counts_ready(3)
    dmesh2 = acc_ref[...] * (1.0 / k_pick)
    ggain_ref[0:1, :] += jnp.sum(dmesh2 * unit2, axis=0, keepdims=True)
    dagg = norm_back(dmesh2, gain2, unit2, scale2).astype(BF16)
    gm_ref[2] += dot_tn(h_high, dagg)
    dhid = dot_nt(dagg, m4_ref[0]) * (1.0 / k_edge)
    dr = (dhid * t_sum).astype(BF16)
    gm_ref[1] += dot_tn(sent, dr)

    def edge_back(k, total):
        rows = pl.ds(pl.multiple_of(k * nodes, nodes), nodes)
        dpre = (dhid * t_ref[rows, :].astype(F32)).astype(BF16)
        return total + dot(eht_ref[:, rows], dpre)

    ds = lax.fori_loop(
        0, k_edge, edge_back, jnp.zeros((table, LATENT), F32), unroll=k_edge
    ).astype(BF16)
    gm_ref[0] += dot_tn(ext_ref[...], ds)
    dext = dot_nt(ds, m2_ref[0])
    dmesh_ref[0] = dmesh2 + dext[:nodes, :] + dot_nt(dr, m3_ref[0])
    dhalo_ref[0] = dext[nodes:, :].astype(BF16)

    @pl.when(member == pl.num_programs(0) - 1)
    def _():
        copy = pltpu.make_async_copy(gm_ref, slots_ref, out_sem)
        copy.start()
        copy.wait()


def main_scratch(k_edge, nodes, points, table):
    return [
        pltpu.VMEM((5, LATENT, LATENT), F32),
        pltpu.SemaphoreType.DMA,
        pltpu.SemaphoreType.DMA((4,)),
        pltpu.VMEM((k_edge * nodes, table), BF16),
        pltpu.VMEM((table, k_edge * nodes), BF16),
        pltpu.VMEM((points, nodes), BF16),
        pltpu.VMEM((nodes, points), BF16),
        pltpu.VMEM((table, LATENT), BF16),
        pltpu.VMEM((k_edge * nodes, LATENT), T_TYPE),
        pltpu.VMEM((nodes, LATENT), BF16),
        pltpu.VMEM((nodes, LATENT), F32),
        pltpu.VMEM((table, LATENT), BF16),
    ]


def whole(shape):
    return pl.BlockSpec(shape, lambda m: (0,) * len(shape))


def per_member(shape):
    return pl.BlockSpec((1,) + shape, lambda m: (m, 0, 0))


def call(kernel, members, in_specs, out_shapes, out_specs, scratch, cost, aliases=None):
    return pl.pallas_call(
        kernel,
        grid=(members,),
        in_specs=in_specs,
        out_shape=out_shapes,
        out_specs=out_specs,
        scratch_shapes=scratch,
        input_output_aliases=aliases or {},
        compiler_params=pltpu.CompilerParams(
            dimension_semantics=("arbitrary",), vmem_limit_bytes=VMEM_BYTES
        ),
        cost_estimate=pl.CostEstimate(flops=cost, bytes_accessed=32 << 20, transcendentals=0),
    )


def shape_of(shape, dtype):
    return jax.ShapeDtypeStruct(shape, dtype)


def slot_of(matrix):
    return 2 * matrix - 5 * ((matrix + 1) // 4)


def neighbours():
    region = lax.axis_index("region")
    slot = lax.rem(region, SLOTS)
    base = region - slot
    one = lax.rem(slot, 2)
    two = lax.rem(slot // 2, 2)
    four = slot // 4
    core = slot + 1 - 2 * one
    side = slot + 2 - 4 * two
    up = slot + 4 - 8 * four
    far = side + 4 - 8 * four
    return base, slot, core, side, up, far


def remote(source, target, send, receive, where):
    return pltpu.make_async_remote_copy(
        src_ref=source, dst_ref=target, send_sem=send, recv_sem=receive,
        device_id=where, device_id_type=MESH,
    )


def greet(places):
    barrier = pltpu.get_barrier_semaphore()
    for place in places:
        pl.semaphore_signal(barrier, inc=1, device_id=place, device_id_type=MESH)
    pl.semaphore_wait(barrier, len(places))


def around():
    region, count = lax.axis_index("region"), lax.axis_size("region")
    following, previous = lax.rem(region + 1, count), lax.rem(region + count - 1, count)
    return {"region": following}, {"region": previous}


def encode_kernel(
    depth, day_ref, matrices_ref, in_ref, outp_ref, gains_ref, dates_ref, valid_ref, x_ref, picks_ref,
    rows_ref, edge_ref, near_ref,
    full_ref, small_out_ref, total_ref, x4_out, a0_out, h1_out, t1_out, unit_out, scale_out, mesh_out,
    sent_out, left_ref, right_ref, eh_out, eht_out, d_out, dt_out,
    edge_cols_ref, grid_cols_ref, eh_ref, eht_ref, d_ref, dt_ref, block_ref, pack_ref, pick_ref, out_ref, x4_ref, xl_ref, a0_ref, h1_ref, t1_ref, unit_ref, scale_ref,
    mesh_ref, sent_ref, buf_ref, w_ref, small_ref, count_ref, counts_ref, sums_ref, heard_ref,
    local_sem, z_send, z_recv, p_send, p_recv, d_send, d_recv, c_send, c_recv, n_send, n_recv,
    s_send, s_recv, w_sem, o_sem, e_send, e_recv, q_sem, b_sem,
):
    base, slot, core, side, up, far = neighbours()
    z = lax.axis_index("row")
    half = block_ref.shape[1] // 2
    low, high = pl.ds(0, half), pl.ds(half, half)
    to_core, to_side, to_up = ({"region": base + place} for place in (core, side, up))
    to_next, to_previous = around()
    to_z = [None] + [{"row": lax.rem(z + d, depth)} for d in range(1, depth)]
    steps = range(1, depth)
    members, variables, points = x_ref.shape
    nodes = a0_ref.shape[1]
    halo = left_ref.shape[1]
    greet(to_z[1:] + [to_core, to_side, to_up, to_next, to_previous])

    def at(d):
        return lax.rem(z + depth - d, depth)

    def arrived(target, receive):
        remote(target, target, receive, receive, to_core).wait_recv()

    def gone(origin, receive):
        remote(origin, origin, receive, receive, to_core).wait_send()

    for k in range(SLOTS - 1):
        block_ref[slot_of(k)] = matrices_ref[k].astype(BF16)
    pack_ref[...] = jnp.zeros_like(pack_ref)
    pack_ref[IN_ROW : IN_ROW + variables, :] = in_ref[...]
    pack_ref[OUT_ROW : OUT_ROW + variables, :] = outp_ref[...]
    pack_ref[GAIN_ROW : GAIN_ROW + gains_ref.shape[0], :] = gains_ref[...]
    pack_ref[DATE_ROW : DATE_ROW + dates_ref.shape[0], :] = dates_ref[...]
    block_ref[SMALL] = jnp.transpose(pack_ref[...]).astype(BF16)
    for d in steps:
        remote(
            block_ref.at[slot], full_ref.at[slot, z], z_send.at[d], z_recv.at[d], to_z[d]
        ).start()
    own = pltpu.make_async_copy(block_ref, full_ref.at[:, z], local_sem)
    own.start()
    valid = jnp.sum(valid_ref[...].astype(F32), axis=1, keepdims=True)
    valid = jnp.sum(valid, axis=0, keepdims=True)
    count_ref[...] = jnp.broadcast_to(valid, count_ref.shape)
    for d in steps:
        remote(count_ref, counts_ref.at[d], n_send.at[d], n_recv.at[d], to_z[d]).start()

    table, k_edge, k_near = eht_ref.shape[0], edge_ref.shape[0], near_ref.shape[0]
    k_grid = picks_ref.shape[0]
    wide = 128
    pieces = nodes // wide
    edge_cols_ref[...] = columns_of(edge_ref[...])
    grid_cols_ref[...] = columns_of(picks_ref[...])

    def build_edges(i, carry):
        k, piece = i // pieces, lax.rem(i, pieces)
        inside = pl.ds(pl.multiple_of(piece * wide, wide), wide)
        across = pl.ds(pl.multiple_of(i * wide, wide), wide)
        columns = edge_cols_ref[inside, :].astype(F32)
        chosen = lax.broadcasted_iota(jnp.int32, columns.shape, 1) == k
        column = jnp.sum(jnp.where(chosen, columns, 0.0), axis=1, keepdims=True).astype(jnp.int32)
        eh_ref[across, :] = count_columns(column, table, 1)
        lines = edge_ref[:, inside].astype(F32)
        chosen = lax.broadcasted_iota(jnp.int32, lines.shape, 0) == k
        line = jnp.sum(jnp.where(chosen, lines, 0.0), axis=0, keepdims=True).astype(jnp.int32)
        eht_ref[:, across] = count_rows(line, table)
        return carry

    def build_near(i, carry):
        inside = pl.ds(pl.multiple_of(i * wide, wide), wide)
        near = near_ref[:, inside]
        d_ref[inside, :] = count_columns(columns_of(near), nodes, k_near)
        dt_ref[:, inside] = count_rows(near, nodes)
        return carry

    def build_grid(i, carry):
        inside = pl.ds(pl.multiple_of(i * 64, 64), 64)
        pick_ref[inside, :] = count_columns(grid_cols_ref[inside, :], points, k_grid)
        return carry

    lax.fori_loop(0, nodes // 64, build_grid, 0)
    out_ref[...] = count_columns(columns_of(rows_ref[...]), nodes, 1)
    edges, nears = k_edge * pieces, points // wide
    share = -(-edges // (depth - 1))

    def from_z(d, carry):
        chunk = full_ref.at[slot, at(d)]
        arrived(chunk, z_recv.at[d])
        remote(chunk, chunk, p_send.at[0, d], p_recv.at[0, d], to_side).start()
        remote(chunk, chunk, p_send.at[1, d], p_recv.at[1, d], to_up).start()
        remote(chunk, chunk, c_send.at[0, d], c_recv.at[0, d], to_core).start()
        lax.fori_loop((d - 1) * share, jnp.minimum(d * share, edges), build_edges, 0)
        return carry

    lax.fori_loop(1, depth, from_z, 0)
    builds = [
        pltpu.make_async_copy(ref, target, b_sem.at[k])
        for k, (ref, target) in enumerate(
            ((eh_ref, eh_out), (eht_ref, eht_out), (d_ref, d_out), (dt_ref, dt_out))
        )
    ]
    builds[0].start()
    builds[1].start()

    total = count_ref[...]
    for d in steps:
        arrived(counts_ref.at[d], n_recv.at[d])
        total = total + counts_ref[d]
    sums_ref[0] = total
    partners = (to_core, to_side, to_up)

    def count_copy(step):
        return remote(
            sums_ref.at[step], heard_ref.at[step], s_send.at[step], s_recv.at[step], partners[step]
        )

    count_copy(0).start()

    def from_sides(d, carry):
        chunk = full_ref.at[side, at(d)]
        arrived(chunk, p_recv.at[0, d])
        part = full_ref.at[side, at(d), low]
        remote(part, part, d_send.at[0, d], d_recv.at[0, d], to_up).start()
        remote(chunk, chunk, c_send.at[1, d], c_recv.at[1, d], to_core).start()
        chunk = full_ref.at[up, at(d)]
        arrived(chunk, p_recv.at[1, d])
        part = full_ref.at[up, at(d), high]
        remote(part, part, d_send.at[1, d], d_recv.at[1, d], to_side).start()
        remote(chunk, chunk, c_send.at[2, d], c_recv.at[2, d], to_core).start()
        return carry

    lax.fori_loop(1, depth, from_sides, 0)

    def gather_inputs(m, carry):
        x4 = dot_nt(pick_ref[...], x_ref[m]) * (1.0 / k_grid)
        top, rest = split_two(x4)
        x4_ref[m] = top
        xl_ref[m] = rest
        return carry

    lax.fori_loop(0, members, gather_inputs, 0)
    for step in (1, 2):
        count_copy(step - 1).wait_recv()
        total = total + heard_ref[step - 1]
        sums_ref[step] = total
        count_copy(step).start()

    def from_far(d, carry):
        arrived(full_ref.at[far, at(d), low], d_recv.at[0, d])
        arrived(full_ref.at[far, at(d), high], d_recv.at[1, d])
        chunk = full_ref.at[far, at(d)]
        remote(chunk, chunk, c_send.at[3, d], c_recv.at[3, d], to_core).start()
        return carry

    lax.fori_loop(1, depth, from_far, 0)
    lax.fori_loop(0, nears, build_near, 0)
    builds[2].start()
    builds[3].start()
    count_copy(2).wait_recv()
    total_ref[...] = total + heard_ref[2]

    def from_core(d, carry):
        for k in range(4):
            arrived(full_ref.at[core, at(d)], c_recv.at[k, d])
        return carry

    lax.fori_loop(1, depth, from_core, 0)
    own.wait()

    loads = [
        pltpu.make_async_copy(full_ref.at[j], w_ref.at[k], w_sem.at[k])
        for k, j in enumerate((SMALL, slot_of(0), slot_of(1)))
    ]
    for copy in loads:
        copy.start()
    for copy in loads:
        copy.wait()
    small_ref[...] = jnp.transpose(w_ref[0].reshape(LATENT, LATENT))
    small_copy = pltpu.make_async_copy(small_ref, small_out_ref, q_sem)
    small_copy.start()
    kept = (
        (x4_ref, x4_out), (a0_ref, a0_out), (h1_ref, h1_out), (t1_ref, t1_out), (unit_ref, unit_out),
        (scale_ref, scale_out), (mesh_ref, mesh_out), (sent_ref, sent_out),
    )

    def kept_copies(m):
        return [
            pltpu.make_async_copy(ref.at[m], target.at[m], o_sem.at[k, m])
            for k, (ref, target) in enumerate(kept)
        ]

    def halo_copies(m):
        return [
            remote(buf_ref.at[m, halo:], left_ref.at[m], e_send.at[0, m], e_recv.at[0, m], to_next),
            remote(buf_ref.at[m, :halo], right_ref.at[m], e_send.at[1, m], e_recv.at[1, m], to_previous),
        ]

    def encode_member(m, carry):
        win = small_ref[IN_ROW : IN_ROW + variables, :]
        agg = dot(x4_ref[m], win) + dot(xl_ref[m], win) + date_row(small_ref, day_ref[m])
        a0 = agg.astype(BF16)
        hid, t1 = silu_parts(0.5 * dot(a0, w_ref[1].reshape(LATENT, LATENT)))
        h1 = hid.astype(BF16)
        unit, scale = normalise(dot(h1, w_ref[2].reshape(LATENT, LATENT)))
        mesh = agg + unit * gain_row(small_ref, 0)
        low_mesh = mesh.astype(BF16)
        buf_ref[m] = dot(out_ref[...], low_mesh).astype(BF16)
        for copy in halo_copies(m):
            copy.start()
        a0_ref[m] = a0
        h1_ref[m] = h1
        t1_ref[m] = t1.astype(BF16)
        unit_ref[m] = unit
        scale_ref[m] = scale
        mesh_ref[m] = mesh
        sent_ref[m] = low_mesh
        for copy in kept_copies(m):
            copy.start()
        return carry

    lax.fori_loop(0, members, encode_member, 0)

    def finish_member(m, carry):
        for copy in halo_copies(m) + kept_copies(m):
            copy.wait()
        return carry

    def finish_row(d, carry):
        gone(block_ref.at[slot], z_send.at[d])
        gone(count_ref, n_send.at[d])
        chunk = full_ref.at[slot, at(d)]
        for k in range(2):
            gone(chunk, p_send.at[k, d])
            gone(full_ref.at[slot, at(d), low], d_send.at[k, d])
        for k in range(4):
            gone(chunk, c_send.at[k, d])
        return carry

    lax.fori_loop(0, members, finish_member, 0)
    lax.fori_loop(1, depth, finish_row, 0)
    for step in range(3):
        count_copy(step).wait_send()
    for copy in builds:
        copy.wait()
    small_copy.wait()


def encode(
    day, matrices, in_proj, out_proj, gains, dates, valid, inputs, picks, rows, edges, near, depth
):
    hbm = pl.BlockSpec(memory_space=pl.ANY)
    vmem = pl.BlockSpec(memory_space=pltpu.VMEM)
    dma = pltpu.SemaphoreType.DMA
    members, variables, points = inputs.shape
    nodes = picks.shape[1]
    halo = rows.shape[1] // 2
    share = matrices.shape[1]
    nodes_of = (members, nodes, LATENT)
    table, pairs = nodes + 2 * halo, edges.shape[0] * nodes
    counts = ((pairs, table), (table, pairs), (points, nodes), (nodes, points))
    kept = [
        ((members, nodes, variables), BF16),
        (nodes_of, BF16),
        (nodes_of, BF16),
        (nodes_of, BF16),
        (nodes_of, F32),
        ((members, nodes, 1), F32),
        (nodes_of, F32),
        (nodes_of, BF16),
    ]
    return pl.pallas_call(
        partial(encode_kernel, depth),
        in_specs=[pl.BlockSpec(memory_space=pltpu.SMEM)] + [vmem] * 11,
        out_shape=[
            shape_of((SLOTS, depth, share, LATENT), BF16),
            shape_of((LATENT, LATENT), BF16),
            shape_of((8, 128), F32),
            *(shape_of(*one) for one in kept),
            shape_of((members, halo, LATENT), BF16),
            shape_of((members, halo, LATENT), BF16),
            *(shape_of(one, BF16) for one in counts),
        ],
        out_specs=[hbm, hbm, vmem] + [hbm] * (len(kept) + 2 + len(counts)),
        scratch_shapes=[
            pltpu.VMEM((nodes, 8), jnp.int32),
            pltpu.VMEM((nodes, 8), jnp.int32),
            *(pltpu.VMEM(one, BF16) for one in counts),
            pltpu.VMEM((SLOTS, share, LATENT), BF16),
            pltpu.VMEM((LATENT, share), F32),
            pltpu.VMEM((nodes, points), BF16),
            pltpu.VMEM((2 * halo, nodes), BF16),
            pltpu.VMEM(*kept[0]),
            *(pltpu.VMEM(*one) for one in kept),
            pltpu.VMEM((members, 2 * halo, LATENT), BF16),
            pltpu.VMEM((3, depth, share, LATENT), BF16),
            pltpu.VMEM((LATENT, LATENT), BF16),
            pltpu.VMEM((8, 128), F32),
            pltpu.VMEM((depth, 8, 128), F32),
            pltpu.VMEM((3, 8, 128), F32),
            pltpu.VMEM((3, 8, 128), F32),
            dma,
            dma((depth,)),
            dma((depth,)),
            dma((2, depth)),
            dma((2, depth)),
            dma((2, depth)),
            dma((2, depth)),
            dma((4, depth)),
            dma((4, depth)),
            dma((depth,)),
            dma((depth,)),
            dma((3,)),
            dma((3,)),
            dma((3,)),
            dma((len(kept), members)),
            dma((2, members)),
            dma((2, members)),
            dma,
            dma((len(counts),)),
        ],
        compiler_params=pltpu.CompilerParams(
            collective_id=0, has_side_effects=True, vmem_limit_bytes=VMEM_BYTES
        ),
    )(
        day, matrices, in_proj, out_proj, gains, dates, valid, inputs, picks, rows, edges, near
    )


def reduce_kernel(
    depth, day_ref, late_ref, momentum_ref, count_ref, dmesh_in, dhalo_ref, rows_ref, x4_in, a0_in,
    h1_in, t1_in, unit_in, scale_in, weights_ref, small_ref, gxd_ref, dsum_ref, gout_ref, ggain_ref,
    loss_ref,
    g_ref, x_ref,
    dmesh_ref, ret_ref, x4_ref, a0_ref, h1_ref, t1_ref, unit_ref, scale_ref, m_ref, back_ref, pack_ref,
    early_ref, own_ref, heard_ref, snd_ref, rcv_ref, snd_low_ref, rcv_low_ref, acc_ref, zr_ref,
    g_own_ref, mb_ref, x_own_ref,
    i_sem, e_send, e_recv, l_sem, h_send, h_recv, p_send, p_recv, q_send, q_recv, z_send, z_recv,
    m_send, m_recv, g_local, g_send, g_recv, x_local, x_send, x_recv,
):
    base, slot, core, side, up, far = neighbours()
    z = lax.axis_index("row")
    rows = acc_ref.shape[0] // depth
    chips = SLOTS // 2
    mine = slot // 2
    parity = lax.rem(slot, 2)
    members, variables = x4_ref.shape[0], x4_ref.shape[2]
    halo = dhalo_ref.shape[1] // 2
    to_core, to_side, to_up, to_far = ({"region": base + place} for place in (core, side, up, far))
    to_next, to_previous = around()
    to_place = (to_far, to_side, to_up)
    places = (far, side, up)
    to_z = [None] + [{"row": lax.rem(z + d, depth)} for d in range(1, depth)]
    greet(to_z[1:] + [to_core, to_side, to_up, to_far, to_next, to_previous])
    sent = []

    def part_of(b):
        return pl.ds(pl.multiple_of(b * rows, rows), rows)

    def send(*args):
        copy = remote(*args)
        copy.start()
        sent.append(copy)

    def arrived(target, receive):
        remote(target, target, receive, receive, to_core).wait_recv()

    def load(*args):
        copy = pltpu.make_async_copy(*args)
        copy.start()
        return copy

    def halo_copies(m):
        return [
            remote(dhalo_ref.at[m, halo:], ret_ref.at[m, :halo], e_send.at[0, m], e_recv.at[0, m], to_next),
            remote(
                dhalo_ref.at[m, :halo], ret_ref.at[m, halo:], e_send.at[1, m], e_recv.at[1, m], to_previous
            ),
        ]

    inner = ((dmesh_in, dmesh_ref), (x4_in, x4_ref), (a0_in, a0_ref), (h1_in, h1_ref), (t1_in, t1_ref),
             (unit_in, unit_ref), (scale_in, scale_ref))

    def inner_loads(m):
        return [
            pltpu.make_async_copy(ref.at[m], target.at[m], i_sem.at[k, m])
            for k, (ref, target) in enumerate(inner)
        ]

    for m in range(members):
        for copy in halo_copies(m):
            copy.start()
    for m in range(members):
        for copy in inner_loads(m):
            copy.start()
    m_loads = []
    first = load(late_ref.at[0], early_ref.at[2], i_sem.at[len(inner), 0])
    for k in range(2):
        m_loads.append(load(weights_ref.at[slot_of(k)], m_ref.at[k], i_sem.at[len(inner), 1 + k]))

    def late_copy(chip):
        return remote(
            late_ref.at[1 + chip], heard_ref.at[chip], h_send.at[chip, 0], h_recv.at[chip, 0], to_core
        )

    def late_load(chip):
        return pltpu.make_async_copy(late_ref.at[1 + chip], own_ref.at[chip], l_sem.at[chip])

    def early_copy(chip, b):
        return remote(
            early_ref.at[chip, part_of(b)], heard_ref.at[chip, part_of(b)], h_send.at[chip, b],
            h_recv.at[chip, b], to_core,
        )

    def low_copy(b):
        return remote(
            snd_low_ref.at[part_of(b)], rcv_low_ref.at[mine, part_of(b)], q_send.at[b], q_recv.at[mine, b],
            {"region": base + SMALL},
        )

    def chip_copy(chip, b):
        return remote(
            snd_ref.at[chip, part_of(b)], rcv_ref.at[mine, part_of(b)], p_send.at[chip, b],
            p_recv.at[mine, b], {"region": base + 2 * chip + parity},
        )

    def pass_on(chip, b, own):
        part = part_of(b)
        total = own[chip, part, :] + heard_ref[chip, part, :]

        @pl.when(mine == chip)
        def _():
            acc_ref[part, :] = total

        @pl.when(mine != chip)
        def _():
            snd_ref[chip, part, :] = total.astype(BF16)
            chip_copy(chip, b).start()

    def pass_late(chip):
        @pl.when(parity == 1)
        def _():
            late_load(chip).wait()
            late_copy(chip).wait_recv()

            def piece(b, carry):
                pass_on(chip, b, own_ref)
                return carry

            lax.fori_loop(0, depth, piece, 0)

    def pass_early(b, carry):
        @pl.when(parity == 0)
        def _():
            def piece(chip, carry):
                early_copy(chip, b).wait_recv()
                pass_on(chip, b, early_ref)
                return carry

            lax.fori_loop(0, chips, piece, 0)
            part = part_of(b)

            @pl.when(mine != SMALL // 2)
            def _():
                total = early_ref[SMALL // 2, part, :] + heard_ref[SMALL // 2, part, :]
                snd_low_ref[part, :] = (total - total.astype(BF16).astype(F32)).astype(BF16)
                low_copy(b).start()

        return carry

    @pl.when(parity == 0)
    def _():
        for chip in range(chips):
            late_copy(chip).start()

    @pl.when(parity == 1)
    def _():
        for chip in range(chips):
            late_load(chip).start()

    lines = lax.broadcasted_iota(jnp.int32, (16, LATENT), 0)
    back_ref[...] = count_rows(rows_ref[...], back_ref.shape[0])
    wout = small_ref[OUT_ROW : OUT_ROW + variables, :]
    pack_ref[...] = jnp.zeros_like(pack_ref)
    top, rest = split_two(gxd_ref[...])
    pack_ref[IN_ROW : IN_ROW + variables, :] = dot(top, wout) + dot(rest, wout)
    pack_ref[OUT_ROW : OUT_ROW + variables, :] = gout_ref[...]
    pack_ref[GAIN_ROW + 1 : GAIN_ROW + 3, :] = ggain_ref[...]
    loss = jnp.sum(loss_ref[...], axis=0, keepdims=True)
    pack_ref[LOSS_ROW : LOSS_ROW + 1, :] = jnp.broadcast_to(loss, (1, LATENT))
    early_ref[0:2] = jnp.zeros((2, LATENT, LATENT), F32)
    for copy in m_loads:
        copy.wait()

    def member_back(m, carry):
        for copy in inner_loads(m):
            copy.wait()
        for copy in halo_copies(m):
            copy.wait()
        dmesh = dmesh_ref[m] + dot(back_ref[...], ret_ref[m])
        unit = unit_ref[m]
        pack_ref[GAIN_ROW : GAIN_ROW + 1, :] += jnp.sum(dmesh * unit, axis=0, keepdims=True)
        dc = norm_back(dmesh, gain_row(small_ref, 0), unit, scale_ref[m]).astype(BF16)
        early_ref[1] += dot_tn(h1_ref[m], dc)
        du = (dot_nt(dc, m_ref[1]) * t1_ref[m].astype(F32)).astype(BF16)
        early_ref[0] += dot_tn(a0_ref[m], du)
        dagg = dmesh + dot_nt(du, m_ref[0])
        pack_ref[IN_ROW : IN_ROW + variables, :] += dot_tn(x4_ref[m], dagg.astype(BF16))
        top, rest = split_two(dsum_ref[m])
        date = jnp.sum(dagg, axis=0, keepdims=True) + dot_tn(top, wout) + dot_tn(rest, wout)
        pack_ref[DATE_ROW : DATE_ROW + 16, :] += jnp.where(lines == day_ref[m], date, 0.0)

        @pl.when(m < chips)
        def _():
            pass_late(m)

        return carry

    lax.fori_loop(0, members, member_back, 0)
    for chip in range(members, chips):
        pass_late(chip)
    early_ref[SMALL // 2] = jnp.transpose(pack_ref[...])
    first.wait()

    @pl.when(parity == 1)
    def _():
        for b in range(depth):
            for chip in range(chips):
                early_copy(chip, b).start()

    lax.fori_loop(0, depth, pass_early, 0)

    sources = [lax.rem(mine + i, chips) for i in range(1, chips)]
    def z_copy(b):
        d = lax.rem(b - z + depth, depth)
        return remote(acc_ref.at[part_of(b)], zr_ref.at[d], z_send.at[b], z_recv.at[d], {"row": b + 0 * z})

    def across_z(b, carry):
        part = part_of(b)
        total = acc_ref[part, :]
        for c in sources:
            arrived(rcv_ref.at[c, part], p_recv.at[c, b])
            total = total + rcv_ref[c, part, :].astype(F32)
        acc_ref[part, :] = total

        @pl.when(slot == SMALL)
        def _():
            low = acc_ref[part, :]
            for c in sources:
                arrived(rcv_low_ref.at[c, part], q_recv.at[c, b])
                low = low + rcv_low_ref[c, part, :].astype(F32)
            acc_ref[part, :] = low

        @pl.when(z != b)
        def _():
            z_copy(b).start()

        return carry

    lax.fori_loop(0, depth, across_z, 0)
    zr_ref[0] = acc_ref[pl.ds(pl.multiple_of(z * rows, rows), rows), :]
    for d in range(1, depth):
        arrived(zr_ref.at[d], z_recv.at[d])
    g_own = zr_ref[z]
    for place in range(1, depth):
        g_own = g_own + zr_ref[lax.rem(z + depth - place, depth)]
    g_own_ref[...] = g_own
    momentum = (
        MUON_MOMENTUM * momentum_ref[mine + (SLOTS // 2 - 1) * parity]
        + (2.0 / count_ref[0:1, 0:1]) * g_own
    )
    mb_ref[0] = momentum.astype(BF16)
    for d in range(1, depth):
        send(mb_ref.at[0], mb_ref.at[d], m_send.at[d], m_recv.at[d], to_z[d])
    g_copy = load(g_own_ref, g_ref.at[slot], g_local)
    for k in range(3):
        send(g_own_ref, g_ref.at[slot], g_send.at[k], g_recv.at[k], to_place[k])
    send(g_own_ref, g_ref.at[slot], g_send.at[3], g_recv.at[3], to_core)

    for d in range(1, depth):
        arrived(mb_ref.at[d], m_recv.at[d])
    everything = jnp.concatenate([mb_ref[d] for d in range(depth)], axis=0)
    wide = everything.astype(F32)
    squares = jnp.sum(jnp.sum(wide * wide, axis=1, keepdims=True), axis=0, keepdims=True)
    inverse = lax.rsqrt(squares + 1e-07)
    turn = momentum * inverse
    current = (wide * inverse).astype(BF16)
    turn_low = turn.astype(BF16)
    for sweep in range(NS_ITERS):
        gram = dot_tn(current, current)
        gram_low = gram.astype(BF16)
        mixing = NS_COEFFS[1] * gram + NS_COEFFS[2] * dot(gram_low, gram_low)
        mixing = mixing.astype(BF16)
        turn = NS_COEFFS[0] * turn + dot(turn_low, mixing)
        turn_low = turn.astype(BF16)
        if sweep < NS_ITERS - 1:
            current = (NS_COEFFS[0] * current.astype(F32) + dot(current, mixing)).astype(BF16)
    x_own_ref[...] = turn_low
    x_copy = pltpu.make_async_copy(x_own_ref, x_ref.at[slot], x_local)
    x_copy.start()
    for k in range(3):
        send(x_own_ref, x_ref.at[slot], x_send.at[k], x_recv.at[k], to_place[k])
    send(x_own_ref, x_ref.at[slot], x_send.at[3], x_recv.at[3], to_core)

    for target, send_sem, recv_sem in ((g_ref, g_send, g_recv), (x_ref, x_send, x_recv)):
        for k in range(3):
            chunk = target.at[places[k]]
            arrived(chunk, recv_sem.at[k])
            send(chunk, chunk, send_sem.at[4 + k], recv_sem.at[4 + k], to_core)
    for target, recv_sem in ((g_ref, g_recv), (x_ref, x_recv)):
        for k in range(3, 7):
            arrived(target.at[core], recv_sem.at[k])
    for copy in sent:
        copy.wait_send()
    @pl.when(parity == 0)
    def _():
        for chip in range(chips):
            late_copy(chip).wait_send()

    @pl.when(parity == 1)
    def _():
        for b in range(depth):
            for chip in range(chips):
                early_copy(chip, b).wait_send()

    for b in range(depth):
        for chip in range(chips):

            @pl.when(mine != chip)
            def _():
                chip_copy(chip, b).wait_send()

        @pl.when((mine != SMALL // 2) & (parity == 0))
        def _():
            low_copy(b).wait_send()

        @pl.when(z != b)
        def _():
            z_copy(b).wait_send()

    g_copy.wait()
    x_copy.wait()


def reduce_gradients(
    day, late, momentum, count, dmesh, dhalo, rows, kept, weights, small, gxd, dsum, gout, ggain, loss,
    depth,
):
    hbm = pl.BlockSpec(memory_space=pl.ANY)
    vmem = pl.BlockSpec(memory_space=pltpu.VMEM)
    dma = pltpu.SemaphoreType.DMA
    members, nodes, width = dmesh.shape
    height = LATENT
    share = height // depth
    halo = dhalo.shape[1]
    chips = SLOTS // 2

    return pl.pallas_call(
        partial(reduce_kernel, depth),
        in_specs=[pl.BlockSpec(memory_space=pltpu.SMEM), hbm, vmem, vmem, hbm, vmem, vmem]
        + [hbm] * len(kept)
        + [hbm]
        + [vmem] * 6,
        out_shape=[
            shape_of((SLOTS, share, width), F32),
            shape_of((SLOTS, share, width), BF16),
        ],
        out_specs=[hbm, hbm],
        scratch_shapes=[
            pltpu.VMEM(dmesh.shape, F32),
            pltpu.VMEM(dhalo.shape, BF16),
            *(pltpu.VMEM(one.shape, one.dtype) for one in kept),
            pltpu.VMEM((2, height, width), BF16),
            pltpu.VMEM((nodes, halo), BF16),
            pltpu.VMEM((height, width), F32),
            pltpu.VMEM((4, height, width), F32),
            pltpu.VMEM((chips, height, width), F32),
            pltpu.VMEM((chips, height, width), F32),
            pltpu.VMEM((chips, height, width), BF16),
            pltpu.VMEM((chips, height, width), BF16),
            pltpu.VMEM((height, width), BF16),
            pltpu.VMEM((chips, height, width), BF16),
            pltpu.VMEM((height, width), F32),
            pltpu.VMEM((depth, share, width), F32),
            pltpu.VMEM((share, width), F32),
            pltpu.VMEM((depth, share, width), BF16),
            pltpu.VMEM((share, width), BF16),
            dma((len(kept) + 2, members)),
            dma((2, members)),
            dma((2, members)),
            dma((chips,)),
            dma((chips, depth)),
            dma((chips, depth)),
            dma((chips, depth)),
            dma((chips, depth)),
            dma((depth,)),
            dma((chips, depth)),
            dma((depth,)),
            dma((depth,)),
            dma((depth,)),
            dma((depth,)),
            dma,
            dma((7,)),
            dma((7,)),
            dma,
            dma((7,)),
            dma((7,)),
        ],
        compiler_params=pltpu.CompilerParams(
            collective_id=1, has_side_effects=True, vmem_limit_bytes=VMEM_BYTES
        ),
    )(
        day, late, momentum, count, dmesh, dhalo, rows, *kept, weights, small, gxd, dsum, gout,
        ggain, loss,
    )


def turn_whole(sums, count, momentum):
    blocks = jnp.stack([sums[slot_of(k)] for k in range(SLOTS - 1)])
    blocks = MUON_MOMENTUM * momentum + (2.0 / count[0, 0]) * blocks
    squares = lax.psum(jnp.sum(blocks * blocks, axis=(1, 2)), "row")
    current = blocks * lax.rsqrt(squares + 1e-07)[:, None, None]

    def product(expression, left, right):
        return jnp.einsum(expression, left, right, precision=lax.Precision.HIGHEST)

    for _ in range(NS_ITERS):
        gram = lax.psum(product("mrk,mrl->mkl", current, current), "row")
        mixing = NS_COEFFS[1] * gram + NS_COEFFS[2] * product("mkj,mjl->mkl", gram, gram)
        current = NS_COEFFS[0] * current + product("mrk,mkl->mrl", current, mixing)
    current = current.astype(BF16)
    by_slot = {slot_of(k): current[k] for k in range(SLOTS - 1)}
    return jnp.stack([by_slot.get(k, current[0]) for k in range(SLOTS)])


def finish_kernel(
    g_ref, rest_ref, x_ref, count_ref, matrix_ref, momentum_ref,
    in_ref, in1_ref, in2_ref, out_ref, out1_ref, out2_ref, gain_ref, gain1_ref, gain2_ref,
    date_ref, date1_ref, date2_ref,
    new_matrix_ref, new_momentum_ref,
    nin_ref, nin1_ref, nin2_ref, nout_ref, nout1_ref, nout2_ref, ngain_ref, ngain1_ref, ngain2_ref,
    ndate_ref, ndate1_ref, ndate2_ref, loss_ref, valid_ref,
):
    scale = 2.0 / count_ref[0:1, 0:1]
    new_momentum_ref[...] = MUON_MOMENTUM * momentum_ref[...] + scale * g_ref[...]
    new_matrix_ref[...] = (
        matrix_ref[...] * (1.0 - MUON_RATE * WEIGHT_DECAY) - MUON_RATE * x_ref[...].astype(F32)
    )

    @pl.when(pl.program_id(0) == 0)
    def _():
        rest = jnp.transpose(rest_ref[0])
        loss_ref[0, 0] = jnp.sum(rest[LOSS_ROW : LOSS_ROW + 1, 0:1])
        valid_ref[0, 0] = jnp.sum(count_ref[0:1, 0:1])
        rest = rest * scale
        for row, rate, decay, old, new in (
            (IN_ROW, MATRIX_RATE, WEIGHT_DECAY, (in_ref, in1_ref, in2_ref), (nin_ref, nin1_ref, nin2_ref)),
            (OUT_ROW, MATRIX_RATE, WEIGHT_DECAY, (out_ref, out1_ref, out2_ref),
             (nout_ref, nout1_ref, nout2_ref)),
            (GAIN_ROW, VECTOR_RATE, 0.0, (gain_ref, gain1_ref, gain2_ref),
             (ngain_ref, ngain1_ref, ngain2_ref)),
            (DATE_ROW, VECTOR_RATE, 0.0, (date_ref, date1_ref, date2_ref),
             (ndate_ref, ndate1_ref, ndate2_ref)),
        ):
            weight, first, second = (ref[...] for ref in old)
            gradient = rest[row : row + weight.shape[0], :]
            for ref, value in zip(new, adam_update(weight, gradient, first, second, rate, decay)):
                ref[...] = value


def finish(sums, turned, count, matrices, momentum, vectors):
    share, width = sums.shape[1:]

    def slot_block():
        return pl.BlockSpec((1, share, width), lambda m: (slot_of(m), 0, 0))

    one = pl.BlockSpec((1, share, width), lambda m: (m, 0, 0))
    return pl.pallas_call(
        finish_kernel,
        grid=(matrices.shape[0],),
        in_specs=[
            slot_block(), pl.BlockSpec((1, share, width), lambda m: (SMALL, 0, 0)), slot_block(),
            whole(count.shape), one, one, *(whole(v.shape) for v in vectors),
        ],
        out_shape=[shape_of(matrices.shape, F32)] * 2
        + [shape_of(v.shape, F32) for v in vectors]
        + [shape_of((1, 1), F32)] * 2,
        out_specs=[one, one] + [whole(v.shape) for v in vectors]
        + [pl.BlockSpec(memory_space=pltpu.SMEM)] * 2,
        compiler_params=pltpu.CompilerParams(
            dimension_semantics=("arbitrary",), vmem_limit_bytes=VMEM_BYTES
        ),
    )(sums, sums, turned, count, matrices, momentum, *vectors)


def adam_update(weight, gradient, first_moment, second_moment, step_rate, decay_rate):
    first_new = BETA_ONE * first_moment + (1.0 - BETA_ONE) * gradient
    second_new = BETA_TWO * second_moment + (1.0 - BETA_TWO) * gradient * gradient
    unbiased_one = first_new / (1.0 - BETA_ONE**STEP)
    unbiased_two = second_new / (1.0 - BETA_TWO**STEP)
    weight_new = weight * (1.0 - step_rate * decay_rate) - step_rate * unbiased_one / (
        jnp.sqrt(unbiased_two) + 1e-08
    )
    return (weight_new, first_new, second_new)


def body(
    inputs,
    targets,
    valid_steps,
    var_weights,
    grid_to_mesh,
    mesh_edges,
    send_rows,
    mesh_to_grid,
    date_index,
    matrices,
    matrices_momentum,
    in_proj,
    in_first,
    in_second,
    out_proj,
    out_first,
    out_second,
    norm_gains,
    gains_first,
    gains_second,
    date_table,
    date_first,
    date_second,
):
    inputs = jnp.swapaxes(inputs, 1, 2)
    targets = jnp.swapaxes(targets, 1, 2)
    members, variables, points = inputs.shape
    nodes = grid_to_mesh.shape[0]
    halo = send_rows.shape[0] // 2
    table = nodes + 2 * halo
    k_edge = mesh_edges.shape[1]
    k_pick = mesh_to_grid.shape[1]
    dates = date_table.shape[0]

    depth = lax.axis_size("row")
    regions = lax.axis_size("region")
    groups = [[g * SLOTS + q for g in range(regions // SLOTS)] for q in range(SLOTS)]
    scalars = pl.BlockSpec(memory_space=pltpu.SMEM)
    hbm = pl.BlockSpec(memory_space=pl.ANY)
    gathered, small, count, *kept, left, right, eh, eht, d, dt = encode(
        date_index, matrices, in_proj, out_proj.T, norm_gains, date_table, valid_steps, inputs,
        grid_to_mesh.T, send_rows[None, :], mesh_edges.T, mesh_to_grid.T, depth,
    )
    mesh1, sent = kept[6:]
    if regions > SLOTS:
        count = lax.psum(count, "region", axis_index_groups=groups)
    weights = gathered.reshape(SLOTS, LATENT, LATENT)
    node_block = per_member((nodes, LATENT))

    def matrix(j):
        place = slot_of(j)
        return pl.BlockSpec(
            (1, LATENT, LATENT), lambda m: (place, 0, 0), pipeline_mode=pl.Buffered(1)
        )

    out_shape = (variables, LATENT)
    late, gout, gxd, dsum, ggain_late, loss_row, dmesh, dhalo = call(
        partial(main_kernel, k_pick),
        members,
        [
            scalars,
            node_block,
            node_block,
            per_member((halo, LATENT)),
            per_member((halo, LATENT)),
            per_member((variables, points)),
            per_member((variables, points)),
            whole((members, points)),
            whole((1, variables)),
            hbm,
            hbm,
            hbm,
            hbm,
            whole((LATENT, LATENT)),
            matrix(2),
            matrix(3),
            matrix(4),
            matrix(5),
            matrix(6),
        ],
        [
            shape_of((5, LATENT, LATENT), F32),
            shape_of(out_shape, F32),
            shape_of((variables, variables), F32),
            shape_of((members, variables, 1), F32),
            shape_of((2, LATENT), F32),
            shape_of((variables, 1), F32),
            shape_of((members, nodes, LATENT), F32),
            shape_of((members, 2 * halo, LATENT), BF16),
        ],
        [
            hbm,
            whole(out_shape),
            whole((variables, variables)),
            per_member((variables, 1)),
            whole((2, LATENT)),
            whole((variables, 1)),
            node_block,
            per_member((2 * halo, LATENT)),
        ],
        main_scratch(k_edge, nodes, points, table),
        60_000_000_000,
    )(
        date_index,
        mesh1,
        sent,
        left,
        right,
        inputs,
        targets,
        valid_steps,
        var_weights[None, :],
        eh,
        eht,
        d,
        dt,
        small,
        weights,
        weights,
        weights,
        weights,
        weights,
    )

    sums, turned = reduce_gradients(
        date_index, late, matrices_momentum, count, dmesh, dhalo, send_rows[None, :], kept[:6], weights,
        small, gxd, dsum, gout, ggain_late, loss_row, depth,
    )
    if regions > SLOTS:
        sums = lax.psum(sums, "region", axis_index_groups=groups)
        turned = turn_whole(sums, count, matrices_momentum)
    vectors = (
        in_proj, in_first, in_second, out_proj.T, out_first.T, out_second.T,
        norm_gains, gains_first, gains_second, date_table, date_first, date_second,
    )
    new = finish(sums, turned, count, matrices, matrices_momentum, vectors)
    return (
        *new[:5],
        *(part.T for part in new[5:8]),
        *new[8:14],
        new[14].reshape(()),
        new[15].reshape(()),
    )


def solution(mesh):
    in_specs = (
        P("row", "region", None),
        P("row", "region", None),
        P("row", "region"),
        P(),
        P("region", None),
        P("region", None),
        P("region"),
        P("region", None),
        P("row"),
        P(None, "row", None),
        P(None, "row", None),
        P(None, "row"),
        P(None, "row"),
        P(None, "row"),
        P("row", None),
        P("row", None),
        P("row", None),
        P(None, "row"),
        P(None, "row"),
        P(None, "row"),
        P(None, "row"),
        P(None, "row"),
        P(None, "row"),
    )
    out_specs = (
        P(None, "row", None),
        P(None, "row", None),
        P(None, "row"),
        P(None, "row"),
        P(None, "row"),
        P("row", None),
        P("row", None),
        P("row", None),
        P(None, "row"),
        P(None, "row"),
        P(None, "row"),
        P(None, "row"),
        P(None, "row"),
        P(None, "row"),
        P(),
        P(),
    )
    return jax.shard_map(body, mesh=mesh, in_specs=in_specs, out_specs=out_specs, check_vma=False)
```

profile of v0, /device:TPU:0, one launch (start us, length us, event | category | flops | bytes accessed | tf_op | source)
XLA Modules:
  0.0 238.4 jit_solution(4621447371390807077)
XLA Ops:
  0.6 50.6 %shard_map.342 = (bf16[8,4,128,512]{3,2,1,0:T(8,128)(2,1)}, bf16[512,512]{1,0:T(8,128)(2,1)}, f32[8,128]{1,0:T(8,128)}, bf16[3,512,227]{2,1,0:T(8,128)(2,1)}, bf...) custom-call(s32[3]{0:T(128)} %day_ref.5, ...), custom_call_target="tpu_custom_call" | custom-call | tf_op jit(solution)/shard_map/pallas_call | solution.py:613
  51.2 86.8 %shard_map.343 = (f32[5,512,512]{2,1,0:T(8,128)}, f32[227,512]{1,0:T(8,128)}, f32[227,227]{1,0:T(8,128)}, f32[3,227,1]{2,1,0:T(8,128)}, f32[2,512]{1,0:T(2,128)}...) custom-call(s32[3]{0:T(128)} %day_ref.5, f32[3,512,512]{2,1,0:T(8,128)} %get-tuple-element.59.mesh_ref, ...), custom_call_target="tpu_custom_call" | custom-call | flops 60000002048 | bytes 33554432 | tf_op jit(solution)/shard_map/pallas_call | solution.py:1205
  138.1 92.1 %shard_map.344 = (f32[8,128,512]{2,1,0:T(8,128)}, bf16[8,128,512]{2,1,0:T(8,128)(2,1)}) custom-call(s32[3]{0:T(128)} %day_ref.5, f32[5,512,512]{2,1,0:T(8,128)} %get-tuple-element.69.late_ref, f32[7,128,512]{2,1,0:T(8,128)} %momentum_ref.3, f32[8,128]{1,0:T(8,128)} %get-tuple-element.70.count_ref, f32[3,512,512]{2,1,0:T(8,128)} %get-tuple-element.71.dmesh_in, ...), custom_call_target="tpu_custom_call" | custom-call | tf_op jit(solution)/shard_map/pallas_call | solution.py:999
  230.2 8.1 %shard_map.345 = (f32[7,128,512]{2,1,0:T(8,128)}, f32[7,128,512]{2,1,0:T(8,128)}, f32[227,128]{1,0:T(8,128)}, f32[227,128]{1,0:T(8,128)}, f32[227,128]{1,0:T(8,1...) custom-call(f32[8,128,512]{2,1,0:T(8,128)} %get-tuple-element.84.g_r, ...), custom_call_target="tpu_custom_call" | custom-call | tf_op jit(solution)/shard_map/pallas_call | solution.py:1119
where the time goes:
time: 239 us; the launch traced here: 238 us
  Pallas kernels  238 us (100%)
    pallas_call x1, Pallas kernels, reduce_gradients(): pl.pallas_call(partial(reduce_kernel, depth), in_specs=[pl.BlockSpec(memo...  92.1 us
    pallas_call x1, Pallas kernels, body(): call(partial(main_kernel, k_pick), members, [scalars, node_block, node_bl...  86.8 us
    pallas_call x1, Pallas kernels, encode(): pl.pallas_call(partial(encode_kernel, depth), in_specs=[pl.BlockSpec(memo...  50.6 us
    pallas_call x1, Pallas kernels, finish(): pl.pallas_call(finish_kernel, grid=(matrices.shape[0],), in_specs=[slot_b...  8.07 us

commit v1 on v0

--- a/solution.py
+++ b/solution.py
@@ -326,7 +326,10 @@
     barrier = pltpu.get_barrier_semaphore()
     for place in places:
         pl.semaphore_signal(barrier, inc=1, device_id=place, device_id_type=MESH)
-    pl.semaphore_wait(barrier, len(places))
+
+
+def greeted(places):
+    pl.semaphore_wait(pltpu.get_barrier_semaphore(), len(places))
 
 
 def around():
@@ -336,14 +339,14 @@
 
 
 def encode_kernel(
-    depth, day_ref, matrices_ref, in_ref, outp_ref, gains_ref, dates_ref, valid_ref, x_ref, picks_ref,
+    depth, day_ref, matrices_ref, in_ref, outp_ref, gains_ref, dates_ref, valid_ref, x_in, picks_ref,
     rows_ref, edge_ref, near_ref,
     full_ref, small_out_ref, total_ref, x4_out, a0_out, h1_out, t1_out, unit_out, scale_out, mesh_out,
     sent_out, left_ref, right_ref, eh_out, eht_out, d_out, dt_out,
-    edge_cols_ref, grid_cols_ref, eh_ref, eht_ref, d_ref, dt_ref, block_ref, pack_ref, pick_ref, out_ref, x4_ref, xl_ref, a0_ref, h1_ref, t1_ref, unit_ref, scale_ref,
+    x_ref, edge_cols_ref, grid_cols_ref, eh_ref, eht_ref, d_ref, dt_ref, block_ref, pack_ref, pick_ref, out_ref, x4_ref, xl_ref, a0_ref, h1_ref, t1_ref, unit_ref, scale_ref,
     mesh_ref, sent_ref, buf_ref, w_ref, small_ref, count_ref, counts_ref, sums_ref, heard_ref,
     local_sem, z_send, z_recv, p_send, p_recv, d_send, d_recv, c_send, c_recv, n_send, n_recv,
-    s_send, s_recv, w_sem, o_sem, e_send, e_recv, q_sem, b_sem,
+    s_send, s_recv, w_sem, o_sem, e_send, e_recv, q_sem, b_sem, x_sem,
 ):
     base, slot, core, side, up, far = neighbours()
     z = lax.axis_index("row")
@@ -353,10 +356,11 @@
     to_next, to_previous = around()
     to_z = [None] + [{"row": lax.rem(z + d, depth)} for d in range(1, depth)]
     steps = range(1, depth)
-    members, variables, points = x_ref.shape
+    members, variables, points = x_in.shape
     nodes = a0_ref.shape[1]
     halo = left_ref.shape[1]
-    greet(to_z[1:] + [to_core, to_side, to_up, to_next, to_previous])
+    peers = to_z[1:] + [to_core, to_side, to_up, to_next, to_previous]
+    greet(peers)
 
     def at(d):
         return lax.rem(z + depth - d, depth)
@@ -366,6 +370,9 @@
 
     def gone(origin, receive):
         remote(origin, origin, receive, receive, to_core).wait_send()
+
+    x_copy = pltpu.make_async_copy(x_in, x_ref, x_sem)
+    x_copy.start()
 
     for k in range(SLOTS - 1):
         block_ref[slot_of(k)] = matrices_ref[k].astype(BF16)
@@ -375,18 +382,8 @@
     pack_ref[GAIN_ROW : GAIN_ROW + gains_ref.shape[0], :] = gains_ref[...]
     pack_ref[DATE_ROW : DATE_ROW + dates_ref.shape[0], :] = dates_ref[...]
     block_ref[SMALL] = jnp.transpose(pack_ref[...]).astype(BF16)
-    for d in steps:
-        remote(
-            block_ref.at[slot], full_ref.at[slot, z], z_send.at[d], z_recv.at[d], to_z[d]
-        ).start()
     own = pltpu.make_async_copy(block_ref, full_ref.at[:, z], local_sem)
     own.start()
-    valid = jnp.sum(valid_ref[...].astype(F32), axis=1, keepdims=True)
-    valid = jnp.sum(valid, axis=0, keepdims=True)
-    count_ref[...] = jnp.broadcast_to(valid, count_ref.shape)
-    for d in steps:
-        remote(count_ref, counts_ref.at[d], n_send.at[d], n_recv.at[d], to_z[d]).start()
-
     table, k_edge, k_near = eht_ref.shape[0], edge_ref.shape[0], near_ref.shape[0]
     k_grid = picks_ref.shape[0]
     wide = 128
@@ -420,10 +417,29 @@
         pick_ref[inside, :] = count_columns(grid_cols_ref[inside, :], points, k_grid)
         return carry
 
+    valid = jnp.sum(valid_ref[...].astype(F32), axis=1, keepdims=True)
+    valid = jnp.sum(valid, axis=0, keepdims=True)
+    count_ref[...] = jnp.broadcast_to(valid, count_ref.shape)
+    out_ref[...] = count_columns(columns_of(rows_ref[...]), nodes, 1)
+    greeted(peers)
+    for d in steps:
+        remote(
+            block_ref.at[slot], full_ref.at[slot, z], z_send.at[d], z_recv.at[d], to_z[d]
+        ).start()
+    for d in steps:
+        remote(count_ref, counts_ref.at[d], n_send.at[d], n_recv.at[d], to_z[d]).start()
+
     lax.fori_loop(0, nodes // 64, build_grid, 0)
-    out_ref[...] = count_columns(columns_of(rows_ref[...]), nodes, 1)
     edges, nears = k_edge * pieces, points // wide
-    share = -(-edges // (depth - 1))
+    first = edges // 4
+    share = -(-(edges - first) // (2 * depth - 2))
+
+    def some_edges(i):
+        return lax.fori_loop(
+            first + i * share, jnp.minimum(first + (i + 1) * share, edges), build_edges, 0
+        )
+
+    lax.fori_loop(0, first, build_edges, 0)
 
     def from_z(d, carry):
         chunk = full_ref.at[slot, at(d)]
@@ -431,7 +447,7 @@
         remote(chunk, chunk, p_send.at[0, d], p_recv.at[0, d], to_side).start()
         remote(chunk, chunk, p_send.at[1, d], p_recv.at[1, d], to_up).start()
         remote(chunk, chunk, c_send.at[0, d], c_recv.at[0, d], to_core).start()
-        lax.fori_loop((d - 1) * share, jnp.minimum(d * share, edges), build_edges, 0)
+        some_edges(d - 1)
         return carry
 
     lax.fori_loop(1, depth, from_z, 0)
@@ -441,8 +457,6 @@
             ((eh_ref, eh_out), (eht_ref, eht_out), (d_ref, d_out), (dt_ref, dt_out))
         )
     ]
-    builds[0].start()
-    builds[1].start()
 
     total = count_ref[...]
     for d in steps:
@@ -469,9 +483,12 @@
         part = full_ref.at[up, at(d), high]
         remote(part, part, d_send.at[1, d], d_recv.at[1, d], to_side).start()
         remote(chunk, chunk, c_send.at[2, d], c_recv.at[2, d], to_core).start()
+        some_edges(depth - 2 + d)
         return carry
 
     lax.fori_loop(1, depth, from_sides, 0)
+    builds[0].start()
+    builds[1].start()
 
     def gather_inputs(m, carry):
         x4 = dot_nt(pick_ref[...], x_ref[m]) * (1.0 / k_grid)
@@ -480,6 +497,7 @@
         xl_ref[m] = rest
         return carry
 
+    x_copy.wait()
     lax.fori_loop(0, members, gather_inputs, 0)
     for step in (1, 2):
         count_copy(step - 1).wait_recv()
@@ -612,7 +630,7 @@
     ]
     return pl.pallas_call(
         partial(encode_kernel, depth),
-        in_specs=[pl.BlockSpec(memory_space=pltpu.SMEM)] + [vmem] * 11,
+        in_specs=[pl.BlockSpec(memory_space=pltpu.SMEM)] + [vmem] * 6 + [hbm] + [vmem] * 4,
         out_shape=[
             shape_of((SLOTS, depth, share, LATENT), BF16),
             shape_of((LATENT, LATENT), BF16),
@@ -624,6 +642,7 @@
         ],
         out_specs=[hbm, hbm, vmem] + [hbm] * (len(kept) + 2 + len(counts)),
         scratch_shapes=[
+            pltpu.VMEM(inputs.shape, BF16),
             pltpu.VMEM((nodes, 8), jnp.int32),
             pltpu.VMEM((nodes, 8), jnp.int32),
             *(pltpu.VMEM(one, BF16) for one in counts),
@@ -659,6 +678,7 @@
             dma((2, members)),
             dma,
             dma((len(counts),)),
+            dma,
         ],
         compiler_params=pltpu.CompilerParams(
             collective_id=0, has_side_effects=True, vmem_limit_bytes=VMEM_BYTES
@@ -669,11 +689,11 @@
 
 
 def reduce_kernel(
-    depth, day_ref, late_ref, momentum_ref, count_ref, dmesh_in, dhalo_ref, rows_ref, x4_in, a0_in,
+    depth, day_ref, late_ref, momentum_in, count_ref, dmesh_in, dhalo_ref, rows_ref, x4_in, a0_in,
     h1_in, t1_in, unit_in, scale_in, weights_ref, small_ref, gxd_ref, dsum_ref, gout_ref, ggain_ref,
     loss_ref,
     g_ref, x_ref,
-    dmesh_ref, ret_ref, x4_ref, a0_ref, h1_ref, t1_ref, unit_ref, scale_ref, m_ref, back_ref, pack_ref,
+    momentum_ref, dmesh_ref, ret_ref, x4_ref, a0_ref, h1_ref, t1_ref, unit_ref, scale_ref, m_ref, back_ref, pack_ref,
     early_ref, own_ref, heard_ref, snd_ref, rcv_ref, snd_low_ref, rcv_low_ref, acc_ref, zr_ref,
     g_own_ref, mb_ref, x_own_ref,
     i_sem, e_send, e_recv, l_sem, h_send, h_recv, p_send, p_recv, q_send, q_recv, z_send, z_recv,
@@ -692,8 +712,12 @@
     to_place = (to_far, to_side, to_up)
     places = (far, side, up)
     to_z = [None] + [{"row": lax.rem(z + d, depth)} for d in range(1, depth)]
-    greet(to_z[1:] + [to_core, to_side, to_up, to_far, to_next, to_previous])
+    peers = to_z[1:] + [to_core, to_side, to_up, to_far, to_next, to_previous]
+    greet(peers)
     sent = []
+
+    def both_ends(i):
+        return lax.rem(i * (depth - 1), depth)
 
     def part_of(b):
         return pl.ds(pl.multiple_of(b * rows, rows), rows)
@@ -729,12 +753,11 @@
         ]
 
     for m in range(members):
-        for copy in halo_copies(m):
-            copy.start()
-    for m in range(members):
         for copy in inner_loads(m):
             copy.start()
-    m_loads = []
+    m_loads = [
+        load(momentum_in.at[mine + (SLOTS // 2 - 1) * parity], momentum_ref, i_sem.at[len(inner) + 1, 0])
+    ]
     first = load(late_ref.at[0], early_ref.at[2], i_sem.at[len(inner), 0])
     for k in range(2):
         m_loads.append(load(weights_ref.at[slot_of(k)], m_ref.at[k], i_sem.at[len(inner), 1 + k]))
@@ -790,7 +813,9 @@
 
             lax.fori_loop(0, depth, piece, 0)
 
-    def pass_early(b, carry):
+    def pass_early(i, carry):
+        b = both_ends(i)
+
         @pl.when(parity == 0)
         def _():
             def piece(chip, carry):
@@ -799,20 +824,15 @@
                 return carry
 
             lax.fori_loop(0, chips, piece, 0)
-            part = part_of(b)
-
-            @pl.when(mine != SMALL // 2)
-            def _():
-                total = early_ref[SMALL // 2, part, :] + heard_ref[SMALL // 2, part, :]
-                snd_low_ref[part, :] = (total - total.astype(BF16).astype(F32)).astype(BF16)
-                low_copy(b).start()
-
-        return carry
-
-    @pl.when(parity == 0)
-    def _():
-        for chip in range(chips):
-            late_copy(chip).start()
+
+        return carry
+
+    def pass_low(b, carry):
+        part = part_of(b)
+        total = early_ref[SMALL // 2, part, :] + heard_ref[SMALL // 2, part, :]
+        snd_low_ref[part, :] = (total - total.astype(BF16).astype(F32)).astype(BF16)
+        low_copy(b).start()
+        return carry
 
     @pl.when(parity == 1)
     def _():
@@ -830,6 +850,16 @@
     loss = jnp.sum(loss_ref[...], axis=0, keepdims=True)
     pack_ref[LOSS_ROW : LOSS_ROW + 1, :] = jnp.broadcast_to(loss, (1, LATENT))
     early_ref[0:2] = jnp.zeros((2, LATENT, LATENT), F32)
+    greeted(peers)
+    for m in range(members):
+        for copy in halo_copies(m):
+            copy.start()
+
+    @pl.when(parity == 0)
+    def _():
+        for chip in range(chips):
+            late_copy(chip).start()
+
     for copy in m_loads:
         copy.wait()
 
@@ -865,18 +895,23 @@
 
     @pl.when(parity == 1)
     def _():
-        for b in range(depth):
+        for i in range(depth):
             for chip in range(chips):
-                early_copy(chip, b).start()
+                early_copy(chip, i * (depth - 1) % depth).start()
 
     lax.fori_loop(0, depth, pass_early, 0)
+
+    @pl.when((mine != SMALL // 2) & (parity == 0))
+    def _():
+        lax.fori_loop(0, depth, pass_low, 0)
 
     sources = [lax.rem(mine + i, chips) for i in range(1, chips)]
     def z_copy(b):
         d = lax.rem(b - z + depth, depth)
         return remote(acc_ref.at[part_of(b)], zr_ref.at[d], z_send.at[b], z_recv.at[d], {"row": b + 0 * z})
 
-    def across_z(b, carry):
+    def across_z(i, carry):
+        b = both_ends(i)
         part = part_of(b)
         total = acc_ref[part, :]
         for c in sources:
@@ -907,7 +942,7 @@
         g_own = g_own + zr_ref[lax.rem(z + depth - place, depth)]
     g_own_ref[...] = g_own
     momentum = (
-        MUON_MOMENTUM * momentum_ref[mine + (SLOTS // 2 - 1) * parity]
+        MUON_MOMENTUM * momentum_ref[...]
         + (2.0 / count_ref[0:1, 0:1]) * g_own
     )
     mb_ref[0] = momentum.astype(BF16)
@@ -998,7 +1033,7 @@
 
     return pl.pallas_call(
         partial(reduce_kernel, depth),
-        in_specs=[pl.BlockSpec(memory_space=pltpu.SMEM), hbm, vmem, vmem, hbm, vmem, vmem]
+        in_specs=[pl.BlockSpec(memory_space=pltpu.SMEM), hbm, hbm, vmem, hbm, vmem, vmem]
         + [hbm] * len(kept)
         + [hbm]
         + [vmem] * 6,
@@ -1008,6 +1043,7 @@
         ],
         out_specs=[hbm, hbm],
         scratch_shapes=[
+            pltpu.VMEM((share, width), F32),
             pltpu.VMEM(dmesh.shape, F32),
             pltpu.VMEM(dhalo.shape, BF16),
             *(pltpu.VMEM(one.shape, one.dtype) for one in kept),
@@ -1026,7 +1062,7 @@
             pltpu.VMEM((share, width), F32),
             pltpu.VMEM((depth, share, width), BF16),
             pltpu.VMEM((share, width), BF16),
-            dma((len(kept) + 2, members)),
+            dma((len(kept) + 3, members)),
             dma((2, members)),
             dma((2, members)),
             dma((chips,)),

time: 239 us -> 234 us (0.979)
  Pallas kernels: 238 us -> 232 us
    pallas_call x1, Pallas kernels: 92.1 us -> 87.2 us  [reduce_gradients(): pl.pallas_call(partial(reduce_kernel, depth), in_specs=[pl.BlockSpec(memo...]
where the time goes in v1:
time: 234 us; the launch traced here: 233 us
  Pallas kernels  232 us (99%)
    pallas_call x1, Pallas kernels, reduce_gradients(): pl.pallas_call(partial(reduce_kernel, depth), in_specs=[pl.BlockSpec(memo...  87.2 us
    pallas_call x1, Pallas kernels, body(): call(partial(main_kernel, k_pick), members, [scalars, node_block, node_bl...  86.8 us
    pallas_call x1, Pallas kernels, encode(): pl.pallas_call(partial(encode_kernel, depth), in_specs=[pl.BlockSpec(memo...  50.1 us
    pallas_call x1, Pallas kernels, finish(): pl.pallas_call(finish_kernel, grid=(matrices.shape[0],), in_specs=[slot_b...  8.07 us

profile of v1, /device:TPU:0, one launch (start us, length us, event | category | flops | bytes accessed | tf_op | source)
XLA Modules:
  0.0 233.1 jit_solution(3028987590134705506)
XLA Ops:
  0.6 50.1 %shard_map.342 = (bf16[8,4,128,512]{3,2,1,0:T(8,128)(2,1)}, bf16[512,512]{1,0:T(8,128)(2,1)}, f32[8,128]{1,0:T(8,128)}, bf16[3,512,227]{2,1,0:T(8,128)(2,1)}, bf...) custom-call(s32[3]{0:T(128)} %day_ref.5, ...), custom_call_target="tpu_custom_call" | custom-call | tf_op jit(solution)/shard_map/pallas_call | solution.py:631
  50.8 86.8 %shard_map.343 = (f32[5,512,512]{2,1,0:T(8,128)}, f32[227,512]{1,0:T(8,128)}, f32[227,227]{1,0:T(8,128)}, f32[3,227,1]{2,1,0:T(8,128)}, f32[2,512]{1,0:T(2,128)}...) custom-call(s32[3]{0:T(128)} %day_ref.5, f32[3,512,512]{2,1,0:T(8,128)} %get-tuple-element.59.mesh_ref, ...), custom_call_target="tpu_custom_call" | custom-call | flops 60000002048 | bytes 33554432 | tf_op jit(solution)/shard_map/pallas_call | solution.py:1241
  137.6 87.2 %shard_map.344 = (f32[8,128,512]{2,1,0:T(8,128)}, bf16[8,128,512]{2,1,0:T(8,128)(2,1)}) custom-call(s32[3]{0:T(128)} %day_ref.5, f32[5,512,512]{2,1,0:T(8,128)} %get-tuple-element.69.late_ref, f32[7,128,512]{2,1,0:T(8,128)} %momentum_ref.1, f32[8,128]{1,0:T(8,128)} %get-tuple-element.70.count_ref, f32[3,512,512]{2,1,0:T(8,128)} %get-tuple-element.71.dmesh_in, ...), custom_call_target="tpu_custom_call" | custom-call | tf_op jit(solution)/shard_map/pallas_call | solution.py:1034
  224.9 8.1 %shard_map.345 = (f32[7,128,512]{2,1,0:T(8,128)}, f32[7,128,512]{2,1,0:T(8,128)}, f32[227,128]{1,0:T(8,128)}, f32[227,128]{1,0:T(8,128)}, f32[227,128]{1,0:T(8,1...) custom-call(f32[8,128,512]{2,1,0:T(8,128)} %get-tuple-element.84.g_r, ...), custom_call_target="tpu_custom_call" | custom-call | tf_op jit(solution)/shard_map/pallas_call | solution.py:1155

commit v2 on v1

--- a/solution.py
+++ b/solution.py
@@ -224,6 +224,12 @@
     lax.fori_loop(0, points // BLOCK, grid_block, 0)
 
     counts_ready(3)
+    decoder_copy = pltpu.make_async_copy(gm_ref.at[3:5], slots_ref.at[3:5], out_sem.at[0])
+
+    @pl.when(member == pl.num_programs(0) - 1)
+    def _():
+        decoder_copy.start()
+
     dmesh2 = acc_ref[...] * (1.0 / k_pick)
     ggain_ref[0:1, :] += jnp.sum(dmesh2 * unit2, axis=0, keepdims=True)
     dagg = norm_back(dmesh2, gain2, unit2, scale2).astype(BF16)
@@ -247,15 +253,16 @@
 
     @pl.when(member == pl.num_programs(0) - 1)
     def _():
-        copy = pltpu.make_async_copy(gm_ref, slots_ref, out_sem)
+        copy = pltpu.make_async_copy(gm_ref.at[0:3], slots_ref.at[0:3], out_sem.at[1])
         copy.start()
         copy.wait()
+        decoder_copy.wait()
 
 
 def main_scratch(k_edge, nodes, points, table):
     return [
         pltpu.VMEM((5, LATENT, LATENT), F32),
-        pltpu.SemaphoreType.DMA,
+        pltpu.SemaphoreType.DMA((2,)),
         pltpu.SemaphoreType.DMA((4,)),
         pltpu.VMEM((k_edge * nodes, table), BF16),
         pltpu.VMEM((table, k_edge * nodes), BF16),
@@ -270,7 +277,7 @@
 
 
 def whole(shape):
-    return pl.BlockSpec(shape, lambda m: (0,) * len(shape))
+    return pl.BlockSpec(shape, lambda m: (0,) * len(shape), pipeline_mode=pl.Buffered(1))
 
 
 def per_member(shape):
@@ -1124,7 +1131,7 @@
         matrix_ref[...] * (1.0 - MUON_RATE * WEIGHT_DECAY) - MUON_RATE * x_ref[...].astype(F32)
     )
 
-    @pl.when(pl.program_id(0) == 0)
+    @pl.when(pl.program_id(0) == pl.num_programs(0) // 2)
     def _():
         rest = jnp.transpose(rest_ref[0])
         loss_ref[0, 0] = jnp.sum(rest[LOSS_ROW : LOSS_ROW + 1, 0:1])

time: 234 us -> 233 us (level)
  no operation moved by 1% of the time
where the time goes in v2:
time: 233 us; the launch traced here: 232 us
  Pallas kernels  231 us (99%)
    pallas_call x1, Pallas kernels, reduce_gradients(): pl.pallas_call(partial(reduce_kernel, depth), in_specs=[pl.BlockSpec(memo...  87.2 us
    pallas_call x1, Pallas kernels, body(): call(partial(main_kernel, k_pick), members, [scalars, node_block, node_bl...  86.2 us
    pallas_call x1, Pallas kernels, encode(): pl.pallas_call(partial(encode_kernel, depth), in_specs=[pl.BlockSpec(memo...  50.1 us
    pallas_call x1, Pallas kernels, finish(): pl.pallas_call(finish_kernel, grid=(matrices.shape[0],), in_specs=[slot_b...  7.75 us

profile of v2, /device:TPU:0, one launch (start us, length us, event | category | flops | bytes accessed | tf_op | source)
XLA Modules:
  0.0 232.1 jit_solution(5496081271441828705)
XLA Ops:
  0.6 50.1 %shard_map.342 = (bf16[8,4,128,512]{3,2,1,0:T(8,128)(2,1)}, bf16[512,512]{1,0:T(8,128)(2,1)}, f32[8,128]{1,0:T(8,128)}, bf16[3,512,227]{2,1,0:T(8,128)(2,1)}, bf...) custom-call(s32[3]{0:T(128)} %day_ref.5, ...), custom_call_target="tpu_custom_call" | custom-call | tf_op jit(solution)/shard_map/pallas_call | solution.py:638
  50.8 86.2 %shard_map.343 = (f32[5,512,512]{2,1,0:T(8,128)}, f32[227,512]{1,0:T(8,128)}, f32[227,227]{1,0:T(8,128)}, f32[3,227,1]{2,1,0:T(8,128)}, f32[2,512]{1,0:T(2,128)}...) custom-call(s32[3]{0:T(128)} %day_ref.5, f32[3,512,512]{2,1,0:T(8,128)} %get-tuple-element.59.mesh_ref, ...), custom_call_target="tpu_custom_call" | custom-call | flops 60000002048 | bytes 33554432 | tf_op jit(solution)/shard_map/pallas_call | solution.py:1248
  137.0 87.2 %shard_map.344 = (f32[8,128,512]{2,1,0:T(8,128)}, bf16[8,128,512]{2,1,0:T(8,128)(2,1)}) custom-call(s32[3]{0:T(128)} %day_ref.5, f32[5,512,512]{2,1,0:T(8,128)} %get-tuple-element.69.late_ref, f32[7,128,512]{2,1,0:T(8,128)} %momentum_ref.1, f32[8,128]{1,0:T(8,128)} %get-tuple-element.70.count_ref, f32[3,512,512]{2,1,0:T(8,128)} %get-tuple-element.71.dmesh_in, ...), custom_call_target="tpu_custom_call" | custom-call | tf_op jit(solution)/shard_map/pallas_call | solution.py:1041
  224.2 7.8 %shard_map.345 = (f32[7,128,512]{2,1,0:T(8,128)}, f32[7,128,512]{2,1,0:T(8,128)}, f32[227,128]{1,0:T(8,128)}, f32[227,128]{1,0:T(8,128)}, f32[227,128]{1,0:T(8,1...) custom-call(f32[8,128,512]{2,1,0:T(8,128)} %get-tuple-element.84.g_r, ...), custom_call_target="tpu_custom_call" | custom-call | tf_op jit(solution)/shard_map/pallas_call | solution.py:1162

commit v3 on v2

--- a/solution.py
+++ b/solution.py
@@ -346,14 +346,14 @@
 
 
 def encode_kernel(
-    depth, day_ref, matrices_ref, in_ref, outp_ref, gains_ref, dates_ref, valid_ref, x_in, picks_ref,
+    depth, day_ref, matrices_ref, in_ref, outp_ref, gains_ref, dates_ref, valid_ref, x_ref, picks_ref,
     rows_ref, edge_ref, near_ref,
     full_ref, small_out_ref, total_ref, x4_out, a0_out, h1_out, t1_out, unit_out, scale_out, mesh_out,
     sent_out, left_ref, right_ref, eh_out, eht_out, d_out, dt_out,
-    x_ref, edge_cols_ref, grid_cols_ref, eh_ref, eht_ref, d_ref, dt_ref, block_ref, pack_ref, pick_ref, out_ref, x4_ref, xl_ref, a0_ref, h1_ref, t1_ref, unit_ref, scale_ref,
+    edge_cols_ref, grid_cols_ref, eh_ref, eht_ref, d_ref, dt_ref, block_ref, pack_ref, pick_ref, out_ref, x4_ref, xl_ref, a0_ref, h1_ref, t1_ref, unit_ref, scale_ref,
     mesh_ref, sent_ref, buf_ref, w_ref, small_ref, count_ref, counts_ref, sums_ref, heard_ref,
     local_sem, z_send, z_recv, p_send, p_recv, d_send, d_recv, c_send, c_recv, n_send, n_recv,
-    s_send, s_recv, w_sem, o_sem, e_send, e_recv, q_sem, b_sem, x_sem,
+    s_send, s_recv, w_sem, o_sem, e_send, e_recv, q_sem, b_sem,
 ):
     base, slot, core, side, up, far = neighbours()
     z = lax.axis_index("row")
@@ -363,7 +363,7 @@
     to_next, to_previous = around()
     to_z = [None] + [{"row": lax.rem(z + d, depth)} for d in range(1, depth)]
     steps = range(1, depth)
-    members, variables, points = x_in.shape
+    members, variables, points = x_ref.shape
     nodes = a0_ref.shape[1]
     halo = left_ref.shape[1]
     peers = to_z[1:] + [to_core, to_side, to_up, to_next, to_previous]
@@ -377,9 +377,6 @@
 
     def gone(origin, receive):
         remote(origin, origin, receive, receive, to_core).wait_send()
-
-    x_copy = pltpu.make_async_copy(x_in, x_ref, x_sem)
-    x_copy.start()
 
     for k in range(SLOTS - 1):
         block_ref[slot_of(k)] = matrices_ref[k].astype(BF16)
@@ -504,7 +501,6 @@
         xl_ref[m] = rest
         return carry
 
-    x_copy.wait()
     lax.fori_loop(0, members, gather_inputs, 0)
     for step in (1, 2):
         count_copy(step - 1).wait_recv()
@@ -637,7 +633,7 @@
     ]
     return pl.pallas_call(
         partial(encode_kernel, depth),
-        in_specs=[pl.BlockSpec(memory_space=pltpu.SMEM)] + [vmem] * 6 + [hbm] + [vmem] * 4,
+        in_specs=[pl.BlockSpec(memory_space=pltpu.SMEM)] + [vmem] * 11,
         out_shape=[
             shape_of((SLOTS, depth, share, LATENT), BF16),
             shape_of((LATENT, LATENT), BF16),
@@ -649,7 +645,6 @@
         ],
         out_specs=[hbm, hbm, vmem] + [hbm] * (len(kept) + 2 + len(counts)),
         scratch_shapes=[
-            pltpu.VMEM(inputs.shape, BF16),
             pltpu.VMEM((nodes, 8), jnp.int32),
             pltpu.VMEM((nodes, 8), jnp.int32),
             *(pltpu.VMEM(one, BF16) for one in counts),
@@ -685,7 +680,6 @@
             dma((2, members)),
             dma,
             dma((len(counts),)),
-            dma,
         ],
         compiler_params=pltpu.CompilerParams(
             collective_id=0, has_side_effects=True, vmem_limit_bytes=VMEM_BYTES

time: 233 us -> 234 us (level)
  no operation moved by 1% of the time
where the time goes in v3:
time: 234 us; the launch traced here: 233 us
  Pallas kernels  232 us (99%)
    pallas_call x1, Pallas kernels, reduce_gradients(): pl.pallas_call(partial(reduce_kernel, depth), in_specs=[pl.BlockSpec(memo...  87.2 us
    pallas_call x1, Pallas kernels, body(): call(partial(main_kernel, k_pick), members, [scalars, node_block, node_bl...  86.2 us
    pallas_call x1, Pallas kernels, encode(): pl.pallas_call(partial(encode_kernel, depth), in_specs=[pl.BlockSpec(memo...  51.1 us
    pallas_call x1, Pallas kernels, finish(): pl.pallas_call(finish_kernel, grid=(matrices.shape[0],), in_specs=[slot_b...  7.75 us

profile of v3, /device:TPU:0, one launch (start us, length us, event | category | flops | bytes accessed | tf_op | source)
XLA Modules:
  0.0 233.1 jit_solution(6407647026914839852)
XLA Ops:
  0.6 51.1 %shard_map.342 = (bf16[8,4,128,512]{3,2,1,0:T(8,128)(2,1)}, bf16[512,512]{1,0:T(8,128)(2,1)}, f32[8,128]{1,0:T(8,128)}, bf16[3,512,227]{2,1,0:T(8,128)(2,1)}, bf...) custom-call(s32[3]{0:T(128)} %day_ref.5, ...), custom_call_target="tpu_custom_call" | custom-call | tf_op jit(solution)/shard_map/pallas_call | solution.py:634
  51.8 86.2 %shard_map.343 = (f32[5,512,512]{2,1,0:T(8,128)}, f32[227,512]{1,0:T(8,128)}, f32[227,227]{1,0:T(8,128)}, f32[3,227,1]{2,1,0:T(8,128)}, f32[2,512]{1,0:T(2,128)}...) custom-call(s32[3]{0:T(128)} %day_ref.5, f32[3,512,512]{2,1,0:T(8,128)} %get-tuple-element.59.mesh_ref, ...), custom_call_target="tpu_custom_call" | custom-call | flops 60000002048 | bytes 33554432 | tf_op jit(solution)/shard_map/pallas_call | solution.py:1242
  138.0 87.2 %shard_map.344 = (f32[8,128,512]{2,1,0:T(8,128)}, bf16[8,128,512]{2,1,0:T(8,128)(2,1)}) custom-call(s32[3]{0:T(128)} %day_ref.5, f32[5,512,512]{2,1,0:T(8,128)} %get-tuple-element.69.late_ref, f32[7,128,512]{2,1,0:T(8,128)} %momentum_ref.1, f32[8,128]{1,0:T(8,128)} %get-tuple-element.70.count_ref, f32[3,512,512]{2,1,0:T(8,128)} %get-tuple-element.71.dmesh_in, ...), custom_call_target="tpu_custom_call" | custom-call | tf_op jit(solution)/shard_map/pallas_call | solution.py:1035
  225.1 7.8 %shard_map.345 = (f32[7,128,512]{2,1,0:T(8,128)}, f32[7,128,512]{2,1,0:T(8,128)}, f32[227,128]{1,0:T(8,128)}, f32[227,128]{1,0:T(8,128)}, f32[227,128]{1,0:T(8,1...) custom-call(f32[8,128,512]{2,1,0:T(8,128)} %get-tuple-element.84.g_r, ...), custom_call_target="tpu_custom_call" | custom-call | tf_op jit(solution)/shard_map/pallas_call | solution.py:1156
